TPU v7x, 128 devices: a whole 4x4x4 slice. The times are simulated.
128 devices in a mesh: face: 32 (over y, x, core), sub: 4 (over z).
Axes of the slice: x: 4, y: 4, z: 4, core: 2. Of those that a mesh axis runs over, the one named last changes fastest.
Arguments:
- h_band: bfloat16 [2, 131072, 256], P(None, ('face', 'sub')), may hold values from -6 to 6
- edges_in: bfloat16 [2, 786432, 256], P(None, ('face', 'sub')), may hold values from -6 to 6
- band_pick: int32 [131072], P(('face', 'sub')), may hold values from 0 to 1023, as said below
- senders: int32 [786432], P(('face', 'sub')), may hold values from 0 to 1279, as said below
- receivers: int32 [786432], P(('face', 'sub')), may hold values from 0 to 1023
- halo_rows: int32 [16384], P(('face', 'sub')), may hold values from 0 to 1023, as said below
- w_edge_in: bfloat16 [768, 256], P(('face', 'sub')), may hold values from -0.21875 to 0.21875
- w_edge_out: bfloat16 [256, 256], P(('face', 'sub')), may hold values from -0.375 to 0.375
- w_node_in: bfloat16 [512, 256], P(('face', 'sub')), may hold values from -0.25 to 0.25
- w_node_out: bfloat16 [256, 256], P(('face', 'sub')), may hold values from -0.375 to 0.375
- biases: bfloat16 [256, 4], P(('face', 'sub')), may hold values from -3 to 3
- norm_gain: bfloat16 [256, 2], P(('face', 'sub')), may hold values from 0.099609375 to 1.8984375
- norm_shift: bfloat16 [256, 2], P(('face', 'sub')), may hold values from -3 to 3
- cot_nodes: bfloat16 [2, 131072, 256], P(None, ('face', 'sub')), may hold values from -6 to 6
- cot_edges: bfloat16 [2, 786432, 256], P(None, ('face', 'sub')), may hold values from -6 to 6
Outputs:
- node_out: bfloat16 [2, 131072, 256], P(None, ('face', 'sub'))
- edge_out: bfloat16 [2, 786432, 256], P(None, ('face', 'sub'))
- grad_nodes: bfloat16 [2, 131072, 256], P(None, ('face', 'sub'))
- grad_edges: bfloat16 [2, 786432, 256], P(None, ('face', 'sub'))
- grad_edge_in: float32 [768, 256], P(('face', 'sub'))
- grad_edge_out: float32 [256, 256], P(('face', 'sub'))
- grad_node_in: float32 [512, 256], P(('face', 'sub'))
- grad_node_out: float32 [256, 256], P(('face', 'sub'))
- grad_biases: float32 [256, 4], P(('face', 'sub'))
- grad_gain: float32 [256, 2], P(('face', 'sub'))
- grad_shift: float32 [256, 2], P(('face', 'sub'))
Inputs may be any that keep to these rules, and one draw needn't show every extreme that they name: `band_pick`: on each device, a permutation of 0 .. 1023. `senders`: rows of the device's table: below 1024 its own nodes, then 128 rows from the previous face device, then 128 from the next. `halo_rows`: on each device, 128 distinct local rows.
All inputs are finite; a program needn't handle non-finite values.
Results may differ from a plain program's by a relative error of at most 0.0079.
Values may be sent and summed in bfloat16 or wider, within the bound.
A program may use at most 256 MiB of HBM per device.

v0:
```python
import jax
import jax.numpy as jnp
from jax import lax
from jax.sharding import PartitionSpec as P

epsilon = 1e-05


def extended(block, sides, width):
    for axis, dim in sides:
        count = lax.axis_size(axis)
        forward = [(i, i + 1) for i in range(count - 1)]
        forward.append((count - 1, 0))
        backward = [(target, source) for source, target in forward]
        low = lax.ppermute(
            lax.slice_in_dim(block, block.shape[dim] - width, None, axis=dim), axis, forward
        )
        high = lax.ppermute(lax.slice_in_dim(block, 0, width, axis=dim), axis, backward)
        block = jnp.concatenate([low, block, high], axis=dim)
    return block


def inner(left, right):
    return lax.dot_general(
        left, right, (((0,), (0,)), ((), ())), preferred_element_type=jnp.float32
    )


def back_dot(grad, weight):
    return lax.dot_general(
        grad, weight, (((1,), (1,)), ((), ())), preferred_element_type=jnp.float32
    )


def forward_dot(values, weight):
    return jnp.dot(values, weight, preferred_element_type=jnp.float32)


def silu_slope(values):
    sigma = jax.nn.sigmoid(values)
    return sigma * (1.0 + values * (1.0 - sigma))


def norm_forward(values, gain, shift):
    center = values - jnp.mean(values, axis=1, keepdims=True)
    spread = lax.rsqrt(jnp.mean(center * center, axis=1, keepdims=True) + epsilon)
    normed = center * spread
    return (normed * gain + shift, normed, spread)


def norm_backward(grad, normed, spread, gain):
    scaled = grad * gain
    inner_mean = jnp.mean(scaled * normed, axis=1, keepdims=True)
    dvalues = spread * (scaled - jnp.mean(scaled, axis=1, keepdims=True) - normed * inner_mean)
    return (dvalues, jnp.sum(grad * normed, axis=0), jnp.sum(grad, axis=0))


def fetch_each(shards):
    return (
        lax.all_gather(shards[0], ("face", "sub"), axis=0, tiled=True),
        lax.all_gather(shards[1], ("face", "sub"), axis=0, tiled=True),
        lax.all_gather(shards[2], ("face", "sub"), axis=0, tiled=True),
        lax.all_gather(shards[3], ("face", "sub"), axis=0, tiled=True),
        lax.all_gather(shards[4], ("face", "sub"), axis=0, tiled=True),
        lax.all_gather(shards[5], ("face", "sub"), axis=0, tiled=True),
        lax.all_gather(shards[6], ("face", "sub"), axis=0, tiled=True),
    )


def body(
    h_band,
    edges_in,
    band_pick,
    senders,
    receivers,
    halo_rows,
    w_edge_in,
    w_edge_out,
    w_node_in,
    w_node_out,
    biases,
    norm_gain,
    norm_shift,
    cot_nodes,
    cot_edges,
):
    shards = (w_edge_in, w_edge_out, w_node_in, w_node_out, biases, norm_gain, norm_shift)
    micro = h_band.shape[0]
    node_dev = h_band.shape[1]
    width = h_band.shape[2]
    halo = halo_rows.shape[0]
    totals = None
    node_list = []
    edge_list = []
    grad_node_list = []
    grad_edge_list = []
    for micro_index in range(micro):
        params = fetch_each(shards)
        wei_in, wei_out, node_wei_in, node_wei_out, bias_all, gain_all, shift_all = params
        bias_all = bias_all.astype(jnp.float32)
        gain_all = gain_all.astype(jnp.float32)
        shift_all = shift_all.astype(jnp.float32)
        edge_rows = edges_in[micro_index]
        h_face = lax.all_to_all(
            h_band[micro_index][band_pick], "face", split_axis=0, concat_axis=0, tiled=True
        )
        padded = extended(h_face[halo_rows], (("face", 0),), halo)
        table = jnp.concatenate([h_face, padded[:halo], padded[2 * halo :]], axis=0)
        joined = jnp.concatenate([table[senders], h_face[receivers], edge_rows], axis=1)
        first = forward_dot(joined, wei_in) + bias_all[:, 0]
        hidden = jax.nn.silu(first).astype(jnp.bfloat16)
        second = forward_dot(hidden, wei_out) + bias_all[:, 1]
        edge_norm, edge_normed, edge_spread = norm_forward(second, gain_all[:, 0], shift_all[:, 0])
        edge_new = (edge_rows.astype(jnp.float32) + edge_norm).astype(jnp.bfloat16)
        summed = jax.ops.segment_sum(
            edge_new.astype(jnp.float32), receivers, num_segments=node_dev
        ).astype(jnp.bfloat16)
        node_joined = jnp.concatenate([h_face, summed], axis=1)
        node_first = forward_dot(node_joined, node_wei_in) + bias_all[:, 2]
        node_hidden = jax.nn.silu(node_first).astype(jnp.bfloat16)
        node_second = forward_dot(node_hidden, node_wei_out) + bias_all[:, 3]
        node_norm, node_normed, node_spread = norm_forward(
            node_second, gain_all[:, 1], shift_all[:, 1]
        )
        node_face = (h_face.astype(jnp.float32) + node_norm).astype(jnp.bfloat16)
        edge_list.append(edge_new)
        returned = lax.all_to_all(node_face, "face", split_axis=0, concat_axis=0, tiled=True)
        node_list.append(jnp.zeros_like(returned).at[band_pick].set(returned))
        grad_face = lax.all_to_all(
            cot_nodes[micro_index][band_pick], "face", split_axis=0, concat_axis=0, tiled=True
        ).astype(jnp.float32)
        dnode_second, grad_gain_node, grad_shift_node = norm_backward(
            grad_face, node_normed, node_spread, gain_all[:, 1]
        )
        dnode_second = dnode_second.astype(jnp.bfloat16)
        grad_out_node = inner(node_hidden, dnode_second)
        dnode_first = (back_dot(dnode_second, node_wei_out) * silu_slope(node_first)).astype(
            jnp.bfloat16
        )
        grad_in_node = inner(node_joined, dnode_first)
        dnode_joined = back_dot(dnode_first, node_wei_in)
        dedge_new = cot_edges[micro_index].astype(jnp.float32) + dnode_joined[:, width:][receivers]
        dsecond, grad_gain_edge, grad_shift_edge = norm_backward(
            dedge_new, edge_normed, edge_spread, gain_all[:, 0]
        )
        dsecond = dsecond.astype(jnp.bfloat16)
        grad_out_edge = inner(hidden, dsecond)
        dfirst = (back_dot(dsecond, wei_out) * silu_slope(first)).astype(jnp.bfloat16)
        grad_in_edge = inner(joined, dfirst)
        djoined = back_dot(dfirst, wei_in)
        grad_edge_list.append((dedge_new + djoined[:, 2 * width :]).astype(jnp.bfloat16))
        dtable = jax.ops.segment_sum(djoined[:, :width], senders, num_segments=node_dev + 2 * halo)
        dface = grad_face + dnode_joined[:, :width] + dtable[:node_dev]
        dface = dface + jax.ops.segment_sum(
            djoined[:, width : 2 * width], receivers, num_segments=node_dev
        )
        dhalo = dtable[node_dev:].astype(jnp.bfloat16)
        came_back = extended(dhalo, (("face", 0),), halo)
        owned = came_back[:halo].astype(jnp.float32) + came_back[3 * halo :].astype(jnp.float32)
        dface = dface.at[halo_rows].add(owned).astype(jnp.bfloat16)
        sent_back = lax.all_to_all(dface, "face", split_axis=0, concat_axis=0, tiled=True)
        grad_node_list.append(jnp.zeros_like(sent_back).at[band_pick].set(sent_back))

        def column_sum(values):
            return jnp.sum(values.astype(jnp.float32), axis=0)

        grads = (
            grad_in_edge,
            grad_out_edge,
            grad_in_node,
            grad_out_node,
            jnp.stack(
                [
                    column_sum(dfirst),
                    column_sum(dsecond),
                    column_sum(dnode_first),
                    column_sum(dnode_second),
                ],
                axis=1,
            ),
            jnp.stack([grad_gain_edge, grad_gain_node], axis=1),
            jnp.stack([grad_shift_edge, grad_shift_node], axis=1),
        )
        shared = (
            lax.psum_scatter(grads[0], ("face", "sub"), scatter_dimension=0, tiled=True),
            lax.psum_scatter(grads[1], ("face", "sub"), scatter_dimension=0, tiled=True),
            lax.psum_scatter(grads[2], ("face", "sub"), scatter_dimension=0, tiled=True),
            lax.psum_scatter(grads[3], ("face", "sub"), scatter_dimension=0, tiled=True),
            lax.psum_scatter(grads[4], ("face", "sub"), scatter_dimension=0, tiled=True),
            lax.psum_scatter(grads[5], ("face", "sub"), scatter_dimension=0, tiled=True),
            lax.psum_scatter(grads[6], ("face", "sub"), scatter_dimension=0, tiled=True),
        )
        totals = shared if totals is None else jax.tree.map(jnp.add, totals, shared)
    return (
        jnp.stack(node_list),
        jnp.stack(edge_list),
        jnp.stack(grad_node_list),
        jnp.stack(grad_edge_list),
        totals[0],
        totals[1],
        totals[2],
        totals[3],
        totals[4],
        totals[5],
        totals[6],
    )


def solution(mesh):
    in_specs = (
        P(None, ("face", "sub"), None),
        P(None, ("face", "sub"), None),
        P(("face", "sub")),
        P(("face", "sub")),
        P(("face", "sub")),
        P(("face", "sub")),
        P(("face", "sub"), None),
        P(("face", "sub"), None),
        P(("face", "sub"), None),
        P(("face", "sub"), None),
        P(("face", "sub"), None),
        P(("face", "sub"), None),
        P(("face", "sub"), None),
        P(None, ("face", "sub"), None),
        P(None, ("face", "sub"), None),
    )
    out_specs = (
        P(None, ("face", "sub"), None),
        P(None, ("face", "sub"), None),
        P(None, ("face", "sub"), None),
        P(None, ("face", "sub"), None),
        P(("face", "sub"), None),
        P(("face", "sub"), None),
        P(("face", "sub"), None),
        P(("face", "sub"), None),
        P(("face", "sub"), None),
        P(("face", "sub"), None),
        P(("face", "sub"), None),
    )
    return jax.shard_map(body, mesh=mesh, in_specs=in_specs, out_specs=out_specs, check_vma=False)
```

profile of v0, /device:TPU:1, one launch (start us, length us, event | category | flops | bytes accessed | tf_op | source)
XLA Modules:
  0.0 1653.7 jit_solution(4883056786264624346)
XLA Ops:
  23.4 47.9 %all-gather.3 = bf16[128,2,2]{2,1,0:T(2,128)(2,1)S(1)} all-gather(bf16[1,2,2]{2,1,0:T(2,128)(2,1)S(1)} %bitcast.236), channel_id=1, replica_groups=mesh['face'=32,'sub'=4] {'face','sub'}, dimensions={0}, use_global_device_ids=true | all-gather | bytes 1032 | tf_op jit(solution)/shard_map/all_gather | solution.py:65
  71.3 44.6 %all-gather.4 = bf16[128,2,2]{2,1,0:T(2,128)(2,1)S(1)} all-gather(bf16[1,2,2]{2,1,0:T(2,128)(2,1)S(1)} %bitcast.237), channel_id=1, replica_groups=mesh['face'=32,'sub'=4] {'face','sub'}, dimensions={0}, use_global_device_ids=true | all-gather | bytes 1032 | tf_op jit(solution)/shard_map/all_gather | solution.py:66
  132.7 49.0 %all-gather.2 = bf16[128,2,256]{2,1,0:T(2,128)(2,1)S(1)} all-gather(bf16[1,2,256]{2,1,0:T(2,128)(2,1)S(1)} %bitcast.226), channel_id=1, replica_groups=mesh['face'=32,'sub'=4] {'face','sub'}, dimensions={0}, use_global_device_ids=true | all-gather | bytes 132096 | tf_op jit(solution)/shard_map/all_gather | solution.py:61
  187.5 50.4 %all-gather.6 = bf16[128,2,256]{2,1,0:T(2,128)(2,1)S(1)} all-gather(bf16[1,2,256]{2,1,0:T(2,128)(2,1)S(1)} %bitcast.227), channel_id=1, replica_groups=mesh['face'=32,'sub'=4] {'face','sub'}, dimensions={0}, use_global_device_ids=true | all-gather | bytes 132096 | tf_op jit(solution)/shard_map/all_gather | solution.py:63
  245.3 44.4 %all-gather.1 = bf16[128,2,4]{2,1,0:T(2,128)(2,1)S(1)} all-gather(bf16[1,2,4]{2,1,0:T(2,128)(2,1)} %bitcast.238), channel_id=1, replica_groups=mesh['face'=32,'sub'=4] {'face','sub'}, dimensions={0}, use_global_device_ids=true | all-gather | bytes 2064 | tf_op jit(solution)/shard_map/all_gather | solution.py:64
  296.4 58.0 %all-gather.5 = bf16[128,4,256]{2,1,0:T(4,128)(2,1)S(1)} all-gather(bf16[1,4,256]{2,1,0:T(4,128)(2,1)S(1)} %bitcast.225), channel_id=1, replica_groups=mesh['face'=32,'sub'=4] {'face','sub'}, dimensions={0}, use_global_device_ids=true | all-gather | bytes 264192 | tf_op jit(solution)/shard_map/all_gather | solution.py:62
  356.5 49.9 %all-gather = bf16[128,6,256]{2,1,0:T(8,128)(2,1)S(1)} all-gather(bf16[1,6,256]{2,1,0:T(8,128)(2,1)} %bitcast.213), channel_id=1, replica_groups=mesh['face'=32,'sub'=4] {'face','sub'}, dimensions={0}, use_global_device_ids=true | all-gather | bytes 396288 | tf_op jit(solution)/shard_map/all_gather | solution.py:60
  457.7 25.3 %gather_fusion.7 = bf16[6144,256]{1,0:T(8,128)(2,1)} fusion(bf16[1024,256]{1,0:T(8,128)(2,1)S(1)} %bitcast.170, s32[6144]{0:T(1024)S(1)} %fusion.58), kind=kCustom, calls=%fused_computation.7 | custom fusion | bytes 6316032 | tf_op jit(solution)/shard_map/gather | solution.py:109
  483.0 25.1 %gather_fusion.3 = bf16[6144,256]{1,0:T(8,128)(2,1)} fusion(bf16[1024,256]{1,0:T(8,128)(2,1)S(1)} %bitcast.175, s32[6144]{0:T(1024)S(1)} %fusion.58), kind=kCustom, calls=%fused_computation.3 | custom fusion | bytes 6316032 | tf_op jit(solution)/shard_map/gather | solution.py:109
  519.8 27.1 %gather_fusion.6 = bf16[6144,256]{1,0:T(8,128)(2,1)} fusion(bf16[1280,256]{1,0:T(8,128)(2,1)S(1)} %pad_maximum_fusion.19, s32[6144]{0:T(1024)} %fusion.57), kind=kCustom, calls=%fused_computation.6 | custom fusion | bytes 6316032 | tf_op jit(solution)/shard_map/gather | solution.py:109
  552.5 27.1 %gather_fusion.2 = bf16[6144,256]{1,0:T(8,128)(2,1)} fusion(bf16[1280,256]{1,0:T(8,128)(2,1)S(1)} %pad_maximum_fusion.18, s32[6144]{0:T(1024)} %fusion.57), kind=kCustom, calls=%fused_computation.2 | custom fusion | bytes 6316032 | tf_op jit(solution)/shard_map/gather | solution.py:109
  620.5 34.4 %scatter_custom_fusion = f32[1024,256]{1,0:T(8,128)S(1)} fusion(s32[6144]{0:T(1024)} %param.19, f32[6144,256]{1,0:T(8,128)} %copy.74, f32[]{:T(128)} %constant.42.clone.1), kind=kCustom, calls=%fused_computation.142 | custom fusion | flops 1572864 | bytes 1049088 | tf_op jit(solution)/shard_map/scatter-add | solution.py:115
  663.3 34.7 %scatter_custom_fusion.2 = f32[1024,256]{1,0:T(8,128)} fusion(s32[6144]{0:T(1024)} %param.19, f32[6144,256]{1,0:T(8,128)} %copy.82, f32[]{:T(128)} %constant.42.clone.1), kind=kCustom, calls=%fused_computation.140 | custom fusion | flops 1572864 | bytes 1049088 | tf_op jit(solution)/shard_map/scatter-add | solution.py:115
  713.5 23.8 %gather_fusion.9 = f32[6144,256]{1,0:T(8,128)} fusion(f32[1024,256]{1,0:T(8,128)S(1)} %slice.181, s32[6144]{0:T(1024)S(1)} %copy-done.42), kind=kCustom, calls=%fused_computation.9 | custom fusion | bytes 12607488 | tf_op jit(solution)/shard_map/gather | solution.py:142
  743.9 9.6 multiply_reduce_fusion.1
  753.5 23.8 %gather_fusion.11 = f32[6144,256]{1,0:T(8,128)} fusion(f32[1024,256]{1,0:T(8,128)S(1)} %slice-done, s32[6144]{0:T(1024)S(1)} %copy-done.42), kind=kCustom, calls=%fused_computation.11 | custom fusion | bytes 12607488 | tf_op jit(solution)/shard_map/gather | solution.py:142
  784.1 12.2 convert_reduce_fusion.2
  824.0 326.8 %fusion = f32[8,256]{1,0:T(8,128)S(1)} fusion(f32[768,256]{1,0:T(8,128)} %fusion.17), kind=kCustom, calls=%all-reduce-scatter | all-reduce-scatter fusion | flops 262145 | bytes 794624
  1164.8 35.3 %scatter_custom_fusion.4 = f32[1280,256]{1,0:T(8,128)} fusion(s32[6144]{0:T(1024)} %param.18, f32[6144,768]{1,0:T(8,128)} %fusion.81, f32[]{:T(128)} %constant.42.clone.1), kind=kCustom, calls=%fused_computation.40 | custom fusion | flops 1572864 | bytes 7602688 | tf_op jit(solution)/shard_map/scatter-add | solution.py:152
  1214.0 35.3 %scatter_custom_fusion.8 = f32[1280,256]{1,0:T(8,128)} fusion(s32[6144]{0:T(1024)} %param.18, f32[6144,768]{1,0:T(8,128)} %fusion.83, f32[]{:T(128)} %constant.42.clone.1), kind=kCustom, calls=%fused_computation.36 | custom fusion | flops 1572864 | bytes 7602688 | tf_op jit(solution)/shard_map/scatter-add | solution.py:152
  1256.5 13.6 all-to-all-start.3
  1347.4 36.3 %scatter_custom_fusion.5 = f32[1024,256]{1,0:T(8,128)} fusion(f32[1024,256]{1,0:T(8,128)} %slice_add_fusion.2, s32[6144]{0:T(1024)} %param.19, f32[6144,768]{1,0:T(8,128)} %fusion.81), kind=kCustom, calls=%fused_computation.38 | custom fusion | flops 1572864 | bytes 7340032 | tf_op jit(solution)/shard_map/scatter-add | solution.py:154
  1433.7 63.6 %all-reduce.8 = (f32[256,4]{0,1:T(4,128)S(1)}, f32[256,2]{0,1:T(2,128)S(1)}, f32[256,2]{0,1:T(2,128)S(1)}) all-reduce(f32[256,4]{0,1:T(4,128)S(1)} %maximum_add_fusion, f32[256,2]{0,1:T(2,128)S(1)} %maximum_add_fusion.1, f32[256,2]{0,1:T(2,128)S(1)} %maximum_add_fusion.2), channel_id=13, replica_groups=mesh['face'=32,'sub'=4] {'face','sub'}, use_global_device_ids=true, to_apply=%region_40.41.clone | all-reduce | flops 2048 | bytes 16384
  1560.2 34.8 %scatter_custom_fusion.9 = f32[1024,256]{1,0:T(8,128)S(1)} fusion(f32[1024,256]{1,0:T(8,128)S(1)} %copy-done.27, s32[6144]{0:T(1024)} %param.19, f32[6144,768]{1,0:T(8,128)} %fusion.83), kind=kCustom, calls=%fused_computation.34 | custom fusion | flops 1572864 | bytes 7340032 | tf_op jit(solution)/shard_map/scatter-add | solution.py:154
  (441 shorter events, 504.6 us)
Async XLA Ops:
  14.7 167.2 %all-to-all-start = ((bf16[32,32,256]{2,1,0:T(8,128)(2,1)}), bf16[32,32,256]{2,1,0:T(8,128)(2,1)S(1)}, u32[]{:S(2)}, u32[]{:S(2)}) async-start(bf16[32,32,256]{2,1,0:T(8,128)(2,1)} %bitcast.1), calls=%async_computation | async-start | bytes 1048576 | tf_op jit(solution)/shard_map/all_to_all | solution.py:104
  181.9 107.9 %all-to-all-start.2 = ((bf16[32,32,256]{2,1,0:T(8,128)(2,1)}), bf16[32,32,256]{2,1,0:T(8,128)(2,1)S(1)}, u32[]{:S(2)}, u32[]{:S(2)}) async-start(bf16[32,32,256]{2,1,0:T(8,128)(2,1)} %bitcast.29), calls=%async_computation.2 | async-start | bytes 1048576 | tf_op jit(solution)/shard_map/all_to_all | solution.py:104
  289.8 140.5 %all-to-all-start.4 = ((bf16[32,32,256]{2,1,0:T(8,128)(2,1)}), bf16[32,32,256]{2,1,0:T(8,128)(2,1)S(1)}, u32[]{:S(2)}, u32[]{:S(2)}) async-start(bf16[32,32,256]{2,1,0:T(8,128)(2,1)} %bitcast.38), calls=%async_computation.4 | async-start | bytes 1048576 | tf_op jit(solution)/shard_map/all_to_all | solution.py:129
  438.0 113.6 %collective-permute-start = (bf16[128,256]{1,0:T(8,128)(2,1)}, bf16[128,256]{1,0:T(8,128)(2,1)}, u32[]{:S(2)}, u32[]{:S(2)}) collective-permute-start(bf16[128,256]{1,0:T(8,128)(2,1)} %gather_fusion.1), channel_id=1, source_target_pairs={{0,4},{4,8},{8,12},{12,16},{16,20},{20,24},{24,28},{28,32},{32,36}... | collective-permute-start | bytes 196616 | tf_op jit(solution)/shard_map/ppermute | solution.py:15
  439.7 112.0 %collective-permute-start.1 = (bf16[128,256]{1,0:T(8,128)(2,1)}, bf16[128,256]{1,0:T(8,128)(2,1)}, u32[]{:S(2)}, u32[]{:S(2)}) collective-permute-start(bf16[128,256]{1,0:T(8,128)(2,1)} %gather_fusion.1), channel_id=1, source_target_pairs={{4,0},{8,4},{12,8},{16,12},{20,16},{24,20},{28,24},{32,28},{36,32}... | collective-permute-start | bytes 196616 | tf_op jit(solution)/shard_map/ppermute | solution.py:18
  440.5 77.7 %collective-permute-start.2 = (bf16[128,256]{1,0:T(8,128)(2,1)S(1)}, bf16[128,256]{1,0:T(8,128)(2,1)S(1)}, u32[]{:S(2)}, u32[]{:S(2)}) collective-permute-start(bf16[128,256]{1,0:T(8,128)(2,1)S(1)} %gather_fusion.5), channel_id=1, source_target_pairs={{0,4},{4,8},{8,12},{12,16},{16,20},{20,24},{24,28},{28,32},{32,36}... | collective-permute-start | bytes 196616 | tf_op jit(solution)/shard_map/ppermute | solution.py:15
  447.8 71.0 %collective-permute-start.3 = (bf16[128,256]{1,0:T(8,128)(2,1)S(1)}, bf16[128,256]{1,0:T(8,128)(2,1)}, u32[]{:S(2)}, u32[]{:S(2)}) collective-permute-start(bf16[128,256]{1,0:T(8,128)(2,1)S(1)} %gather_fusion.5), channel_id=1, source_target_pairs={{4,0},{8,4},{12,8},{16,12},{20,16},{24,20},{28,24},{32,28},{36,32}... | collective-permute-start | bytes 196616 | tf_op jit(solution)/shard_map/ppermute | solution.py:18
  1151.4 176.1 %collective-permute-start.38 = (f32[8,256]{1,0:T(8,128)S(1)}, f32[8,256]{1,0:T(8,128)S(1)}, u32[]{:S(2)}, u32[]{:S(2)}) collective-permute-start(f32[8,256]{1,0:T(8,128)S(1)} %fusion), channel_id=1, source_target_pairs={{0,31},{1,32},{2,33},{3,34},{4,35},{5,36},{6,37},{7,38},{8,39},{9,... | collective-permute-start | bytes 24584
  1152.7 180.6 %collective-permute-start.37 = (f32[8,256]{1,0:T(8,128)S(1)}, f32[8,256]{1,0:T(8,128)}, u32[]{:S(2)}, u32[]{:S(2)}) collective-permute-start(f32[8,256]{1,0:T(8,128)S(1)} %fusion), channel_id=1, source_target_pairs={{0,30},{1,31},{2,32},{3,33},{4,34},{5,35},{6,36},{7,37},{8,38},{9,... | collective-permute-start | bytes 24584
  1154.6 183.9 %collective-permute-start.36 = (f32[8,256]{1,0:T(8,128)S(1)}, f32[8,256]{1,0:T(8,128)}, u32[]{:S(2)}, u32[]{:S(2)}) collective-permute-start(f32[8,256]{1,0:T(8,128)S(1)} %fusion), channel_id=1, source_target_pairs={{0,29},{1,30},{2,31},{3,32},{4,33},{5,34},{6,35},{7,36},{8,37},{9,... | collective-permute-start | bytes 24584
  1256.5 60.9 %all-to-all-start.3 = ((bf16[32,32,256]{2,1,0:T(8,128)(2,1)}), bf16[32,32,256]{2,1,0:T(8,128)(2,1)}, u32[]{:S(2)}, u32[]{:S(2)}) async-start(bf16[32,32,256]{2,1,0:T(8,128)(2,1)} %bitcast.193), calls=%async_computation.3 | async-start | bytes 1048576 | tf_op jit(solution)/shard_map/all_to_all | solution.py:127
  1270.1 360.7 %all-reduce.12.cloned.1.call-start = ((), (), s32[]{:S(2)}) async-start(), calls=%async_computation.8 | async-start | bytes 2097152
  1317.4 87.3 %all-to-all-start.1 = ((bf16[32,32,256]{2,1,0:T(8,128)(2,1)}), bf16[32,32,256]{2,1,0:T(8,128)(2,1)S(1)}, u32[]{:S(2)}, u32[]{:S(2)}) async-start(bf16[32,32,256]{2,1,0:T(8,128)(2,1)} %bitcast.192), calls=%async_computation.1 | async-start | bytes 1048576 | tf_op jit(solution)/shard_map/all_to_all | solution.py:127
  1327.5 61.8 %collective-permute-start.35 = (f32[8,256]{1,0:T(8,128)S(1)}, f32[8,256]{1,0:T(8,128)S(1)}, u32[]{:S(2)}, u32[]{:S(2)}) collective-permute-start(f32[8,256]{1,0:T(8,128)S(1)} %fusion), channel_id=1, source_target_pairs={{0,28},{1,29},{2,30},{3,31},{4,32},{5,33},{6,34},{7,35},{8,36},{9,... | collective-permute-start | bytes 24584
  1404.7 205.9 %all-to-all-start.5 = ((bf16[32,32,256]{2,1,0:T(8,128)(2,1)}), bf16[32,32,256]{2,1,0:T(8,128)(2,1)S(1)}, u32[]{:S(2)}, u32[]{:S(2)}) async-start(bf16[32,32,256]{2,1,0:T(8,128)(2,1)} %bitcast.41), calls=%async_computation.5 | async-start | bytes 1048576 | tf_op jit(solution)/shard_map/all_to_all | solution.py:161
  1408.9 88.4 %collective-permute-start.25 = (f32[8,256]{1,0:T(8,128)S(1)}, f32[8,256]{1,0:T(8,128)S(1)}, u32[]{:S(2)}, u32[]{:S(2)}) collective-permute-start(f32[8,256]{1,0:T(8,128)S(1)} %fusion), channel_id=1, source_target_pairs={{0,18},{1,19},{2,20},{3,21},{4,22},{5,23},{6,24},{7,25},{8,26},{9,... | collective-permute-start | bytes 24584
  1414.1 86.0 %collective-permute-start.24 = (f32[8,256]{1,0:T(8,128)S(1)}, f32[8,256]{1,0:T(8,128)S(1)}, u32[]{:S(2)}, u32[]{:S(2)}) collective-permute-start(f32[8,256]{1,0:T(8,128)S(1)} %fusion), channel_id=1, source_target_pairs={{0,17},{1,18},{2,19},{3,20},{4,21},{5,22},{6,23},{7,24},{8,25},{9,... | collective-permute-start | bytes 24584
  1417.2 86.6 %collective-permute-start.23 = (f32[8,256]{1,0:T(8,128)S(1)}, f32[8,256]{1,0:T(8,128)S(1)}, u32[]{:S(2)}, u32[]{:S(2)}) collective-permute-start(f32[8,256]{1,0:T(8,128)S(1)} %fusion), channel_id=1, source_target_pairs={{0,16},{1,17},{2,18},{3,19},{4,20},{5,21},{6,22},{7,23},{8,24},{9,... | collective-permute-start | bytes 24584
  1421.9 87.0 %collective-permute-start.22 = (f32[8,256]{1,0:T(8,128)S(1)}, f32[8,256]{1,0:T(8,128)S(1)}, u32[]{:S(2)}, u32[]{:S(2)}) collective-permute-start(f32[8,256]{1,0:T(8,128)S(1)} %fusion), channel_id=1, source_target_pairs={{0,15},{1,16},{2,17},{3,18},{4,19},{5,20},{6,21},{7,22},{8,23},{9,... | collective-permute-start | bytes 24584
  1427.7 83.7 %collective-permute-start.21 = (f32[8,256]{1,0:T(8,128)S(1)}, f32[8,256]{1,0:T(8,128)S(1)}, u32[]{:S(2)}, u32[]{:S(2)}) collective-permute-start(f32[8,256]{1,0:T(8,128)S(1)} %fusion), channel_id=1, source_target_pairs={{0,14},{1,15},{2,16},{3,17},{4,18},{5,19},{6,20},{7,21},{8,22},{9,... | collective-permute-start | bytes 24584
  1532.1 71.5 %collective-permute-start.10 = (f32[8,256]{1,0:T(8,128)S(1)}, f32[8,256]{1,0:T(8,128)S(1)}, u32[]{:S(2)}, u32[]{:S(2)}) collective-permute-start(f32[8,256]{1,0:T(8,128)S(1)} %fusion), channel_id=1, source_target_pairs={{0,3},{1,4},{2,5},{3,6},{4,7},{5,8},{6,9},{7,10},{8,11},{9,12},{10... | collective-permute-start | bytes 24584
  1536.6 67.0 %collective-permute-start.9 = (f32[8,256]{1,0:T(8,128)S(1)}, f32[8,256]{1,0:T(8,128)S(1)}, u32[]{:S(2)}, u32[]{:S(2)}) collective-permute-start(f32[8,256]{1,0:T(8,128)S(1)} %fusion), channel_id=1, source_target_pairs={{0,2},{1,3},{2,4},{3,5},{4,6},{5,7},{6,8},{7,9},{8,10},{9,11},{10,... | collective-permute-start | bytes 24584
  1539.5 64.1 %collective-permute-start.8 = (f32[8,256]{1,0:T(8,128)S(1)}, f32[8,256]{1,0:T(8,128)S(1)}, u32[]{:S(2)}, u32[]{:S(2)}) collective-permute-start(f32[8,256]{1,0:T(8,128)S(1)} %fusion), channel_id=1, source_target_pairs={{0,1},{1,2},{2,3},{3,4},{4,5},{5,6},{6,7},{7,8},{8,9},{9,10},{10,1... | collective-permute-start | bytes 24584
  1547.8 60.1 %collective-permute-start.6 = (bf16[128,256]{1,0:T(8,128)(2,1)S(1)}, bf16[128,256]{1,0:T(8,128)(2,1)S(1)}, u32[]{:S(2)}, u32[]{:S(2)}) collective-permute-start(bf16[128,256]{1,0:T(8,128)(2,1)S(1)} %get-tuple-element.88), channel_id=1, source_target_pairs={{0,4},{4,8},{8,12},{12,16},{16,20},{20,24},{24,28},{28,32},{32,36}... | collective-permute-start | bytes 196616 | tf_op jit(solution)/shard_map/ppermute | solution.py:15
  (127 other events, 4816.5 us)
Sparse Core Ops, SparseCore 0:
  1314.8 150.9 all-reduce.11
where the time goes:
time: 1670 us; the launch traced here: 1650 us
  blocking collectives  735 us (44%)
  local copies, waits for them, and re-layouts  345 us (21%)
  other arithmetic  290 us (17%)
  starting transfers between devices  198 us (12%)
  matrix products  69.6 us (4%)
    unnamed x2, blocking collectives  390 us
    unnamed x33, starting transfers between devices  119 us
    unnamed x234, local copies, waits for them, and re-layouts  79.4 us
    scatter-add x2, other arithmetic, body(): jax.ops.segment_sum(djoined[:, width:2 * width], receivers, num_segments=...  71.1 us
    scatter-add x2, other arithmetic, body(): jax.ops.segment_sum(djoined[:, :width], senders, num_segments=node_dev +...  70.6 us
    scatter-add x2, other arithmetic, body(): jax.ops.segment_sum(edge_new.astype(jnp.float32), receivers, num_segments...  69.1 us
    gather x4, local copies, waits for them, and re-layouts, body(): table[senders]  63.6 us
    gather x4, local copies, waits for them, and re-layouts, body(): dnode_joined[:, width:][receivers]  60.9 us
  transfers between devices with their start and end apart: 49, of which 0 were waited for; matrix products, arithmetic and copies ran while one was open for 25% of the time, Pallas kernels for 0%

commit v1 on v0

v1 whole, which is shorter than its diff:
```python
import functools

import jax
import jax.numpy as jnp
from jax import lax
from jax.experimental import pallas as pl
from jax.experimental.pallas import tpu as pltpu
from jax.sharding import PartitionSpec as P

F32, BF = jnp.float32, jnp.bfloat16
EPS = 1e-05
MESH = pl.DeviceIdType.MESH
VMEM = pl.BlockSpec(memory_space=pltpu.VMEM)
ANY = pl.BlockSpec(memory_space=pl.ANY)


def dot(a, b):
    return jnp.dot(a, b, preferred_element_type=F32)


def dot_nt(a, b):
    return lax.dot_general(a, b, (((1,), (1,)), ((), ())), preferred_element_type=F32)


def dot_tn(a, b):
    return lax.dot_general(a, b, (((0,), (0,)), ((), ())), preferred_element_type=F32)


def onehot(col, count):
    lane = lax.broadcasted_iota(jnp.int32, col.shape, 1)
    parts = [(col == lane + 128 * k).astype(F32).astype(BF) for k in range(count // 128)]
    return jnp.concatenate(parts, axis=1)


def onehot_t(row, count):
    spot = lax.broadcasted_iota(jnp.int32, (count, row.shape[1]), 0)
    return (spot == row).astype(F32).astype(BF)


def column(row):
    return jnp.broadcast_to(row, (128, 128)).T


def colsum(values):
    return jnp.sum(values, axis=0, keepdims=True)


def greet(faces, subs):
    me_f, me_s = lax.axis_index("face"), lax.axis_index("sub")
    barrier = pltpu.get_barrier_semaphore()

    def face_signal(k, carry):
        pl.semaphore_signal(
            barrier, inc=1, device_id=(lax.rem(me_f + k, faces), me_s), device_id_type=MESH
        )
        return carry

    def sub_signal(k, carry):
        pl.semaphore_signal(
            barrier, inc=1, device_id=(me_f, lax.rem(me_s + k, subs)), device_id_type=MESH
        )
        return carry

    lax.fori_loop(1, faces, face_signal, 0)
    lax.fori_loop(1, subs, sub_signal, 0)
    pl.semaphore_wait(barrier, faces + subs - 2)


class Spread:
    def __init__(self, axis, count, size, src, dst, send, recv):
        self.axis, self.count, self.size = axis, count, size
        self.src, self.dst, self.send, self.recv = src, dst, send, recv

    def copy(self, k):
        me_f, me_s = lax.axis_index("face"), lax.axis_index("sub")
        me = me_f if self.axis == "face" else me_s
        peer = lax.rem(me + k, self.count)
        device = (peer, me_s) if self.axis == "face" else (me_f, peer)
        rows = pl.ds(pl.multiple_of(me * self.size, self.size), self.size)
        return pltpu.make_async_remote_copy(
            src_ref=self.src(peer),
            dst_ref=self.dst.at[rows],
            send_sem=self.send.at[k],
            recv_sem=self.recv.at[k],
            device_id=device,
            device_id_type=MESH,
        )

    def start(self):
        def go(k, carry):
            self.copy(k).start()
            return carry

        lax.fori_loop(1, self.count, go, 0)

    def wait_recv(self):
        def go(k, carry):
            self.copy(k).wait_recv()
            return carry

        lax.fori_loop(1, self.count, go, 0)

    def wait_send(self):
        def go(k, carry):
            self.copy(k).wait_send()
            return carry

        lax.fori_loop(1, self.count, go, 0)


def block_of(ref, size):
    return lambda peer: ref.at[pl.ds(pl.multiple_of(peer * size, size), size)]


def shift_copies(src, dst, half, faces, sems):
    me_f, me_s = lax.axis_index("face"), lax.axis_index("sub")
    up, down = lax.rem(me_f + 1, faces), lax.rem(me_f + faces - 1, faces)
    return [
        pltpu.make_async_remote_copy(
            src_ref=src[i],
            dst_ref=dst.at[pl.ds(i * half, half)],
            send_sem=sems.at[2 * i],
            recv_sem=sems.at[2 * i + 1],
            device_id=((up, down)[i], me_s),
            device_id_type=MESH,
        )
        for i in range(2)
    ]


def in_kernel(
    faces, subs,
    h_band, cot, pick, halo_rows, wei_s, weo_s, wni_s, wno_s, bias_s, gain_s, shift_s,
    h_face, g_face, halo, wei, weo, wni, wno, small,
    hcat, hpick, gpick, pcol, pack, wz, wall, wide, stage, bound,
    z_send, z_recv, w_send, w_recv, h_send, h_recv, g_send, g_recv, b_sem,
):
    me_f, me_s = lax.axis_index("face"), lax.axis_index("sub")
    nodes, two = h_face.shape
    width = two // 2
    share = nodes // faces
    ra, rb, rc = wei_s.shape[0], weo_s.shape[0], wni_s.shape[0]
    rows = ra + 3 * rb + rc
    devices = faces * subs
    half = halo_rows.shape[1]

    pack[...] = jnp.zeros_like(pack)
    pack[0:ra, :] = wei_s[...].astype(F32)
    pack[ra : ra + rb, :] = weo_s[...].astype(F32)
    pack[ra + rb : ra + rb + rc, :] = wni_s[...].astype(F32)
    pack[ra + rb + rc : ra + 2 * rb + rc, :] = wno_s[...].astype(F32)
    pack[ra + 2 * rb + rc :, 0:4] = bias_s[...].astype(F32)
    pack[ra + 2 * rb + rc :, 4:6] = gain_s[...].astype(F32)
    pack[ra + 2 * rb + rc :, 6:8] = shift_s[...].astype(F32)
    mine = pl.ds(pl.multiple_of(me_s * rows, rows), rows)
    wz[mine, :] = pack[...].astype(BF)
    z_move = Spread("sub", subs, rows, lambda peer: wz.at[mine], wz, z_send, z_recv)
    size_w = subs * rows
    w_move = Spread("face", faces, size_w, lambda peer: wz, wall, w_send, w_recv)
    h_move = Spread("face", faces, share, block_of(hpick, share), h_face, h_send, h_recv)
    g_move = Spread("face", faces, share, block_of(gpick, share), g_face, g_send, g_recv)

    def make_col(j, carry):
        pcol[pl.ds(pl.multiple_of(j * 128, 128), 128), :] = column(pick[pl.ds(j, 1), :])
        return carry

    lax.fori_loop(0, nodes // 128, make_col, 0)
    block = min(256, nodes)

    def select(src, dst):
        for m in range(2):
            hcat[:, m * width : (m + 1) * width] = src[m]

        def go(i, carry):
            at = pl.ds(pl.multiple_of(i * block, block), block)
            dst[at, :] = dot(onehot(pcol[at, :], nodes), hcat[...]).astype(BF)
            return carry

        lax.fori_loop(0, nodes // block, go, 0)

    own = pl.ds(pl.multiple_of(me_f * share, share), share)
    select(h_band, hpick)
    greet(faces, subs)
    z_move.start()
    h_move.start()
    h_face[own, :] = hpick[own, :]
    z_move.wait_recv()
    w_move.start()
    wall[pl.ds(pl.multiple_of(me_f * size_w, size_w), size_w), :] = wz[...]
    select(cot, gpick)
    g_move.start()
    g_face[own, :] = gpick[own, :]
    h_move.wait_recv()
    hcol = column(halo_rows[...])
    bound[...] = dot(onehot(hcol, nodes), h_face[...]).astype(BF)
    b_move = shift_copies((bound, bound), halo, half, faces, b_sem)
    for one in b_move:
        one.start()
    w_move.wait_recv()
    for c in range(width // 128):
        wide[c] = wall[:, c * 128 : (c + 1) * 128].astype(F32)
    low, high = 0, ra
    for out, count in ((wei, ra), (weo, rb), (wni, rc), (wno, rb)):
        for i in range(count):
            for c in range(width // 128):
                stage[c, pl.ds(i, devices, stride=count), :] = wide[
                    c, pl.ds(low + i, devices, stride=rows), :
                ]
        for c in range(width // 128):
            out[:, c * 128 : (c + 1) * 128] = stage[c, 0 : devices * count, :].astype(BF)
        low += count
    total = jnp.zeros((128, width), F32)
    for i in range(rb):
        part = wide[0, pl.ds(low + i, devices, stride=rows), :].astype(BF)
        spot = lax.broadcasted_iota(jnp.int32, (devices, width), 1)
        source = lax.broadcasted_iota(jnp.int32, (devices, width), 0)
        total += dot_tn(part, (spot == source * rb + i).astype(F32).astype(BF))
    small[...] = total[0:8, :]
    g_move.wait_recv()
    for one in b_move:
        one.wait_recv()
        one.wait_send()
    for move in (z_move, h_move, w_move, g_move):
        move.wait_send()


def gather_in(faces, subs, h_band, cot, pick, halo_rows, shards):
    nodes, width = h_band.shape[1:]
    half = halo_rows.shape[1]
    counts = [s.shape[0] for s in shards[:4]]
    rows = sum(counts) + counts[1]
    devices = faces * subs
    S = jax.ShapeDtypeStruct
    two = 2 * width
    sem = pltpu.SemaphoreType.DMA
    return pl.pallas_call(
        functools.partial(in_kernel, faces, subs),
        out_shape=(
            S((nodes, two), BF), S((nodes, two), BF), S((2 * half, two), BF),
            *[S((c * devices, width), BF) for c in counts], S((8, width), F32),
        ),
        in_specs=[VMEM] * 11,
        out_specs=tuple([VMEM] * 8),
        scratch_shapes=[
            pltpu.VMEM((nodes, two), BF), pltpu.VMEM((nodes, two), BF), pltpu.VMEM((nodes, two), BF),
            pltpu.VMEM((nodes, 128), jnp.int32),
            pltpu.VMEM((rows, width), F32), pltpu.VMEM((subs * rows, width), BF),
            pltpu.VMEM((devices * rows, width), BF), pltpu.VMEM((width // 128, devices * rows, 128), F32),
            pltpu.VMEM((width // 128, max(counts) * devices, 128), F32), pltpu.VMEM((half, two), BF),
            sem((subs,)), sem((subs,)), sem((faces,)), sem((faces,)),
            sem((faces,)), sem((faces,)), sem((faces,)), sem((faces,)), sem((4,)),
        ],
        compiler_params=pltpu.CompilerParams(
            collective_id=0, has_side_effects=True, vmem_limit_bytes=40 * 1024 * 1024
        ),
        name="gather_in",
    )(h_band, cot, pick, halo_rows, *shards)


def compute_kernel(
    tile,
    h, halo, g, wei, weo, wni, wno, small, send, recv, edges, cot,
    eo_out, ge_out, nf_out, df_out, dhalo_out, gwei, gweo, gwni, gwno, gsmall,
    e_v, c_v, o_v, slope_v, hid_v, y_v, q_v, scol, rcol, pq, summed, ss, sr, dsum, sems,
):
    count, width = edges.shape[1:]
    nodes = h.shape[0]
    table = nodes + halo.shape[0]
    for m in range(2):
        pltpu.make_async_copy(edges.at[m], e_v.at[m], sems.at[m]).start()
        pltpu.make_async_copy(cot.at[m], c_v.at[m], sems.at[2 + m]).start()

    def make_col(j, carry):
        for src, dst in ((send, scol), (recv, rcol)):
            dst[pl.ds(pl.multiple_of(j * 128, 128), 128), :] = column(src[pl.ds(j, 1), :])
        return carry

    lax.fori_loop(0, count // 128, make_col, 0)
    for ref in (gwei, gweo, gwni, gwno, gsmall):
        ref[...] = jnp.zeros_like(ref)
    b0, b1, b2, b3, gn0, gn1, sh0, sh1 = (small[k : k + 1, :] for k in range(8))
    per = tile // 128

    def index_row(ref, i):
        return jnp.concatenate([ref[pl.ds(i * per + k, 1), :] for k in range(per)], axis=1)

    for m in range(2):
        lanes = slice(m * width, (m + 1) * width)
        hm = h[:, lanes]
        pq[0:nodes, :] = dot(hm, wei[0:width, :]).astype(BF)
        pq[nodes:table, :] = dot(halo[:, lanes], wei[0:width, :]).astype(BF)
        pq[table:, :] = dot(hm, wei[width : 2 * width, :]).astype(BF)
        summed[...] = jnp.zeros_like(summed)
        pltpu.make_async_copy(edges.at[m], e_v.at[m], sems.at[m]).wait()

        def forward(i, carry):
            rows = pl.ds(pl.multiple_of(i * tile, tile), tile)
            e = e_v[m, rows, :]
            first = dot(e, wei[2 * width :, :]) + b0
            first += dot(onehot(scol[rows, :], table), pq[0:table, :])
            first += dot(onehot(rcol[rows, :], nodes), pq[table:, :])
            s = jax.nn.sigmoid(first)
            slope_v[rows, :] = (s * (1.0 + first * (1.0 - s))).astype(BF)
            hidden = (first * s).astype(BF)
            hid_v[rows, :] = hidden
            second = dot(hidden, weo[...]) + b1
            center = second - jnp.mean(second, axis=1, keepdims=True)
            q = lax.rsqrt(jnp.mean(center * center, axis=1, keepdims=True) + EPS)
            y = center * q
            y_v[rows, :] = y.astype(BF)
            q_v[rows, :] = jnp.broadcast_to(q, (tile, 128))
            eo = (e.astype(F32) + (y * gn0 + sh0)).astype(BF)
            o_v[m, rows, :] = eo
            summed[...] += dot(onehot_t(index_row(recv, i), nodes), eo)
            return carry

        lax.fori_loop(0, count // tile, forward, 0)
        pltpu.make_async_copy(o_v.at[m], eo_out.at[m], sems.at[4 + m]).start()
        sm = summed[...].astype(BF)
        nfirst = dot(hm, wni[0:width, :]) + dot(sm, wni[width:, :]) + b2
        sigma = jax.nn.sigmoid(nfirst)
        nhid = (nfirst * sigma).astype(BF)
        second = dot(nhid, wno[...]) + b3
        center = second - jnp.mean(second, axis=1, keepdims=True)
        q = lax.rsqrt(jnp.mean(center * center, axis=1, keepdims=True) + EPS)
        y = center * q
        nf_out[:, lanes] = (hm.astype(F32) + (y * gn1 + sh1)).astype(BF)
        gf = g[:, lanes].astype(F32)
        scaled = gf * gn1
        m1 = jnp.mean(scaled, axis=1, keepdims=True)
        m2 = jnp.mean(scaled * y, axis=1, keepdims=True)
        dn2 = (q * (scaled - m1 - y * m2)).astype(BF)
        slope = sigma * (1.0 + nfirst * (1.0 - sigma))
        dn1 = (dot_nt(dn2, wno[...]) * slope).astype(BF)
        gwno[...] += dot_tn(nhid, dn2)
        gwni[0:width, :] += dot_tn(hm, dn1)
        gwni[width:, :] += dot_tn(sm, dn1)
        gsmall[2:3, :] += colsum(dn1.astype(F32))
        gsmall[3:4, :] += colsum(dn2.astype(F32))
        gsmall[5:6, :] += colsum(gf * y)
        gsmall[7:8, :] += colsum(gf)
        df_out[:, lanes] = gf + dot_nt(dn1, wni[0:width, :])
        dsum[...] = dot_nt(dn1, wni[width:, :]).astype(BF)
        ss[...] = jnp.zeros_like(ss)
        sr[...] = jnp.zeros_like(sr)
        pltpu.make_async_copy(cot.at[m], c_v.at[m], sems.at[2 + m]).wait()

        def backward(i, carry):
            db2, dgain, dshift = carry
            rows = pl.ds(pl.multiple_of(i * tile, tile), tile)
            de = c_v[m, rows, :].astype(F32) + dot(onehot(rcol[rows, :], nodes), dsum[...])
            y = y_v[rows, :].astype(F32)
            scaled = de * gn0
            m1 = jnp.mean(scaled, axis=1, keepdims=True)
            m2 = jnp.mean(scaled * y, axis=1, keepdims=True)
            de2 = (q_v[rows, 0:1] * (scaled - m1 - y * m2)).astype(BF)
            dgain = dgain + colsum(de * y)
            dshift = dshift + colsum(de)
            db2 = db2 + colsum(de2.astype(F32))
            gweo[...] += dot_tn(hid_v[rows, :], de2)
            de1 = (dot_nt(de2, weo[...]) * slope_v[rows, :].astype(F32)).astype(BF)
            gwei[2 * width :, :] += dot_tn(e_v[m, rows, :], de1)
            c_v[m, rows, :] = (de + dot_nt(de1, wei[2 * width :, :])).astype(BF)
            ss[...] += dot(onehot_t(index_row(send, i), table), de1)
            sr[...] += dot(onehot_t(index_row(recv, i), nodes), de1)
            return db2, dgain, dshift

        zero = jnp.zeros((1, width), F32)
        db2, dgain, dshift = lax.fori_loop(0, count // tile, backward, (zero, zero, zero))
        pltpu.make_async_copy(c_v.at[m], ge_out.at[m], sems.at[6 + m]).start()
        gsmall[1:2, :] += db2
        gsmall[4:5, :] += dgain
        gsmall[6:7, :] += dshift
        gsmall[0:1, :] += colsum(sr[...])
        sb = ss[...].astype(BF)
        rb = sr[...].astype(BF)
        gwei[0:width, :] += dot_tn(hm, sb[0:nodes]) + dot_tn(halo[:, lanes], sb[nodes:])
        gwei[width : 2 * width, :] += dot_tn(hm, rb)
        df_out[:, lanes] += dot_nt(sb[0:nodes], wei[0:width, :]) + dot_nt(rb, wei[width : 2 * width, :])
        dhalo_out[:, lanes] = dot_nt(sb[nodes:], wei[0:width, :]).astype(BF)
    for m in range(2):
        pltpu.make_async_copy(o_v.at[m], eo_out.at[m], sems.at[4 + m]).wait()
        pltpu.make_async_copy(c_v.at[m], ge_out.at[m], sems.at[6 + m]).wait()


def compute(h, halo, g, params, send, recv, edges, cot):
    nodes = h.shape[0]
    count, width = edges.shape[1:]
    table = nodes + halo.shape[0]
    tile = min(1024, count)
    S = jax.ShapeDtypeStruct
    V = pltpu.VMEM
    return pl.pallas_call(
        functools.partial(compute_kernel, tile),
        out_shape=(
            S((2, count, width), BF), S((2, count, width), BF), S((nodes, 2 * width), BF),
            S((nodes, 2 * width), F32), S((halo.shape[0], 2 * width), BF),
            S((3 * width, width), F32), S((width, width), F32), S((2 * width, width), F32),
            S((width, width), F32), S((8, width), F32),
        ),
        in_specs=[VMEM] * 10 + [ANY] * 2,
        out_specs=tuple([ANY] * 2 + [VMEM] * 8),
        scratch_shapes=[
            V((2, count, width), BF), V((2, count, width), BF), V((2, count, width), BF),
            V((count, width), BF), V((count, width), BF), V((count, width), BF), V((count, 128), F32),
            V((count, 128), jnp.int32), V((count, 128), jnp.int32),
            V((table + nodes, width), BF), V((nodes, width), F32), V((table, width), F32),
            V((nodes, width), F32), V((nodes, width), BF), pltpu.SemaphoreType.DMA((8,)),
        ],
        compiler_params=pltpu.CompilerParams(vmem_limit_bytes=62 * 1024 * 1024),
        name="compute",
    )(h, halo, g, *params, send, recv, edges, cot)


def out_kernel(
    faces, subs, counts,
    nf, df, dhalo, halo_rows, gwei, gweo, gwni, gwno, gsmall,
    nf_got, df_got, parts,
    dsend, back, stage, pack, zsrc, zgot, fsum, tall, flat,
    b_sem, n_send, n_recv, d_send, d_recv, z_send, z_recv, f_send, f_recv,
):
    me_f, me_s = lax.axis_index("face"), lax.axis_index("sub")
    nodes, two = nf.shape
    width = two // 2
    share = nodes // faces
    half = halo_rows.shape[1]
    rows = sum(counts) + counts[1]
    size_z = faces * rows
    own = pl.ds(pl.multiple_of(me_f * share, share), share)

    greet(faces, subs)
    b_move = shift_copies(
        (dhalo.at[pl.ds(half, half)], dhalo.at[pl.ds(0, half)]), back, half, faces, b_sem
    )
    for one in b_move:
        one.start()
    n_move = Spread("face", faces, share, block_of(nf, share), nf_got, n_send, n_recv)
    n_move.start()
    nf_got[own, :] = nf[own, :]
    tall[...] = jnp.zeros_like(tall)
    tall[0:8, :] = gsmall[...]
    flat[...] = tall[...].T
    pack[...] = jnp.zeros_like(pack)
    low = 0
    for ref, count in zip((gwei, gweo, gwni, gwno), counts):
        for c in range(width // 128):
            lanes = slice(c * 128, (c + 1) * 128)
            stage[0 : ref.shape[0], :] = ref[:, lanes]
            for s in range(subs):
                for i in range(count):
                    pack[c, pl.ds(s * size_z + low + i, faces, stride=rows), :] = stage[
                        pl.ds(s * count + i, faces, stride=subs * count), :
                    ]
        low += count
    for s in range(subs):
        for i in range(counts[1]):
            pack[0, pl.ds(s * size_z + low + i, faces, stride=rows), :] = flat[
                pl.ds(s * counts[1] + i, faces, stride=subs * counts[1]), :
            ]
    for c in range(width // 128):
        zsrc[:, c * 128 : (c + 1) * 128] = pack[c].astype(BF)
    z_move = Spread("sub", subs, size_z, block_of(zsrc, size_z), zgot, z_send, z_recv)
    z_move.start()
    mine = pl.ds(pl.multiple_of(me_s * size_z, size_z), size_z)
    zgot[mine, :] = zsrc[mine, :]
    spread = lax.broadcasted_iota(jnp.int32, (nodes, half), 0)
    place = (spread == halo_rows[...]).astype(F32).astype(BF)
    for one in b_move:
        one.wait_recv()
    for m in range(2):
        lanes = slice(m * width, (m + 1) * width)
        owned = dot(place, back[0:half, lanes]) + dot(place, back[half : 2 * half, lanes])
        dsend[:, lanes] = (df[:, lanes] + owned).astype(BF)
    d_move = Spread("face", faces, share, block_of(dsend, share), df_got, d_send, d_recv)
    d_move.start()
    df_got[own, :] = dsend[own, :]
    z_move.wait_recv()
    total = zgot[0:size_z, :].astype(F32)
    for s in range(1, subs):
        total += zgot[s * size_z : (s + 1) * size_z, :].astype(F32)
    fsum[...] = total
    f_move = Spread("face", faces, rows, block_of(fsum, rows), parts, f_send, f_recv)
    f_move.start()
    slot = pl.ds(pl.multiple_of(me_f * rows, rows), rows)
    parts[slot, :] = fsum[slot, :]
    for move in (n_move, d_move, f_move):
        move.wait_recv()
    for one in b_move:
        one.wait_send()
    for move in (n_move, z_move, d_move, f_move):
        move.wait_send()


def send_out(faces, subs, counts, nf, df, dhalo, halo_rows, grads):
    nodes, two = nf.shape
    width = two // 2
    half = halo_rows.shape[1]
    rows = sum(counts) + counts[1]
    S, V = jax.ShapeDtypeStruct, pltpu.VMEM
    sem = pltpu.SemaphoreType.DMA
    size_z = faces * rows
    return pl.pallas_call(
        functools.partial(out_kernel, faces, subs, counts),
        out_shape=(S((nodes, two), BF), S((nodes, two), BF), S((size_z, width), F32)),
        in_specs=[VMEM] * 9,
        out_specs=(VMEM, VMEM, VMEM),
        scratch_shapes=[
            V((nodes, two), BF), V((2 * half, two), BF), V((counts[0] * faces * subs, 128), F32),
            V((width // 128, subs * size_z, 128), F32), V((subs * size_z, width), BF), V((subs * size_z, width), BF), V((size_z, width), F32),
            V((128, width), F32), V((width, 128), F32),
            sem((4,)), sem((faces,)), sem((faces,)), sem((faces,)), sem((faces,)),
            sem((subs,)), sem((subs,)), sem((faces,)), sem((faces,)),
        ],
        compiler_params=pltpu.CompilerParams(
            collective_id=1, has_side_effects=True, vmem_limit_bytes=40 * 1024 * 1024
        ),
        name="send_out",
    )(nf, df, dhalo, halo_rows, *grads)


def final_kernel(
    faces, counts, nf_got, df_got, parts, pick,
    node_out, grad_nodes, o0, o1, o2, o3, o4, o5, o6,
):
    nodes, two = nf_got.shape
    width = two // 2
    index = jnp.concatenate([pick[k : k + 1, :] for k in range(nodes // 128)], axis=1)
    block = min(256, nodes)
    for b in range(nodes // block):
        spot = lax.broadcasted_iota(jnp.int32, (block, nodes), 0) + b * block
        place = (spot == index).astype(F32).astype(BF)
        rows = pl.ds(b * block, block)
        for src, out in ((nf_got, node_out), (df_got, grad_nodes)):
            moved = dot(place, src[...]).astype(BF)
            for m in range(2):
                out[m, rows, :] = moved[:, m * width : (m + 1) * width]
    rows = sum(counts) + counts[1]
    total = parts[0:rows, :]
    for p in range(1, faces):
        total += parts[p * rows : (p + 1) * rows, :]
    at = 0
    for out, count in zip((o0, o1, o2, o3), counts):
        out[...] = total[at : at + count, :]
        at += count
    o4[...] = total[at:, 0:4]
    o5[...] = total[at:, 4:6]
    o6[...] = total[at:, 6:8]


def finish(faces, counts, nf_got, df_got, parts, pick):
    nodes, two = nf_got.shape
    width = two // 2
    S = jax.ShapeDtypeStruct
    return pl.pallas_call(
        functools.partial(final_kernel, faces, counts),
        out_shape=(
            S((2, nodes, width), BF), S((2, nodes, width), BF),
            *[S((c, width), F32) for c in counts],
            S((counts[1], 4), F32), S((counts[1], 2), F32), S((counts[1], 2), F32),
        ),
        in_specs=[VMEM] * 4,
        out_specs=tuple([VMEM] * 9),
        compiler_params=pltpu.CompilerParams(vmem_limit_bytes=40 * 1024 * 1024),
        name="finish",
    )(nf_got, df_got, parts, pick)


def body(
    faces, subs,
    h_band, edges_in, band_pick, senders, receivers, halo_rows,
    w_edge_in, w_edge_out, w_node_in, w_node_out, biases, norm_gain, norm_shift,
    cot_nodes, cot_edges,
):
    pick = band_pick.reshape(-1, 128)
    offered = halo_rows.reshape(1, -1)
    send = senders.reshape(-1, 128)
    recv = receivers.reshape(-1, 128)
    shards = (w_edge_in, w_edge_out, w_node_in, w_node_out, biases, norm_gain, norm_shift)
    counts = tuple(s.shape[0] for s in shards[:4])
    h, g, halo, *params = gather_in(faces, subs, h_band, cot_nodes, pick, offered, shards)
    edge_out, grad_edges, nf, df, dhalo, *grads = compute(
        h, halo, g, params, send, recv, edges_in, cot_edges
    )
    nf_got, df_got, parts = send_out(faces, subs, counts, nf, df, dhalo, offered, grads)
    node_out, grad_nodes, *weights = finish(faces, counts, nf_got, df_got, parts, pick)
    return (node_out, edge_out, grad_nodes, grad_edges, *weights)


def solution(mesh):
    both = ("face", "sub")
    rows, items = P(both, None), P(None, both, None)
    in_specs = (items, items, P(both), P(both), P(both), P(both)) + (rows,) * 7 + (items, items)
    out_specs = (items,) * 4 + (rows,) * 7
    return jax.shard_map(
        functools.partial(body, mesh.shape["face"], mesh.shape["sub"]),
        mesh=mesh, in_specs=in_specs, out_specs=out_specs, check_vma=False,
    )
```

time: 1670 us -> 225 us (0.13)
  blocking collectives: 735 us -> 0 us
  local copies, waits for them, and re-layouts: 345 us -> 23 us
  other arithmetic: 290 us -> 0 us
  Pallas kernels: 0 us -> 200 us
  starting transfers between devices: 198 us -> 0 us
  matrix products: 69.6 us -> 0 us
    unnamed x2 -> x0, blocking collectives: 390 us -> none
    all_gather x7 -> x0, blocking collectives: 344 us -> none  [the longest x1 58 us: fetch_each(): lax.all_gather(shards[2], ('face', 'sub'), axis=0, tiled=True)]
    scatter-add x8 -> x0, other arithmetic: 216 us -> none  [the longest x2 71.1 us: body(): jax.ops.segment_sum(djoined[:, width:2 * width], receivers, num_segments=...]
    gather x18 -> x0, local copies, waits for them, and re-layouts: 207 us -> none  [the longest x4 63.6 us: body(): table[senders]]
    pallas_call x0 -> x4, Pallas kernels: none -> 200 us  [the longest x1 105 us: compute(): pl.pallas_call(functools.partial(compute_kernel, tile), out_shape=(S((2,...]
    unnamed x33 -> x0, starting transfers between devices: 119 us -> none
    dot_general x24 -> x0, matrix products: 69.6 us -> none  [the longest x8 30.3 us: back_dot(): lax.dot_general(grad, weight, (((1,), (1,)), ((), ())), preferred_element...]
    all_to_all x8 -> x0, starting transfers between devices: 58.4 us -> none  [the longest x2 20 us: body(): lax.all_to_all(node_face, 'face', split_axis=0, concat_axis=0, tiled=True)]
  transfers between devices with their start and end apart: 49 -> 0, of which waited for: 0 -> 0; matrix products, arithmetic and copies ran while one was open for 25% -> 0% of each run, Pallas kernels for 0% -> 0%
where the time goes in v1:
time: 225 us; the launch traced here: 224 us
  Pallas kernels  200 us (89%)
  local copies, waits for them, and re-layouts  23 us (10%)
    pallas_call x1, Pallas kernels, compute(): pl.pallas_call(functools.partial(compute_kernel, tile), out_shape=(S((2,...  105 us
    pallas_call x1, Pallas kernels, gather_in(): pl.pallas_call(functools.partial(in_kernel, faces, subs), out_shape=(S((n...  51.7 us
    pallas_call x1, Pallas kernels, send_out(): pl.pallas_call(functools.partial(out_kernel, faces, subs, counts), out_sh...  39.7 us
    unnamed x58, local copies, waits for them, and re-layouts  23 us

profile of v1, /device:TPU:1, one launch (start us, length us, event | category | flops | bytes accessed | tf_op | source)
XLA Modules:
  0.0 223.8 jit_solution(4766012982186844120)
XLA Ops:
  0.7 1.2 copy-done.3
  1.9 1.2 copy-done.4
  3.1 0.7 copy-done.16
  3.8 0.7 copy-done.20
  4.5 0.7 copy-done.21
  5.8 0.7 copy-done.24
  6.5 0.7 copy-done.25
  9.1 51.7 %gather_in.1 = (bf16[1024,512]{1,0:T(8,128)(2,1)S(1)}, bf16[1024,512]{1,0:T(8,128)(2,1)S(1)}, bf16[256,512]{1,0:T(8,128)(2,1)S(1)}, bf16[768,256]{1,0:T(8,128)(2...) custom-call(bf16[2,1024,256]{2,1,0:T(8,128)(2,1)S(1)} %copy-done.3, ...), custom_call_target="tpu_custom_call" | custom-call | tf_op jit(solution)/shard_map/gather_in/pallas_call | solution.py:236
  60.8 1.0 copy-done.1
  61.8 1.0 copy-done.2
  62.8 0.7 copy-done.8
  63.5 0.7 copy-done.9
  64.2 0.7 copy-done.10
  66.8 105.2 %compute.1 = (bf16[2,6144,256]{2,1,0:T(8,128)(2,1)}, bf16[2,6144,256]{2,1,0:T(8,128)(2,1)}, bf16[1024,512]{1,0:T(8,128)(2,1)}, f32[1024,512]{1,0:T(8,128)}, bf16...) custom-call(bf16[1024,512]{1,0:T(8,128)(2,1)} %copy-done.1, ...), custom_call_target="tpu_custom_call" | custom-call | tf_op jit(solution)/shard_map/compute/pallas_call | solution.py:393
  172.1 1.6 copy-done
  173.7 1.2 copy-done.5
  174.9 1.1 copy-done.6
  176.1 1.0 copy-done.7
  177.1 0.9 copy-done.11
  178.1 0.9 copy-done.12
  179.0 0.9 copy-done.13
  180.0 0.7 copy-done.18
  180.7 39.7 %send_out.1 = (bf16[1024,512]{1,0:T(8,128)(2,1)S(1)}, bf16[1024,512]{1,0:T(8,128)(2,1)S(1)}, f32[512,256]{1,0:T(8,128)S(1)}) custom-call(bf16[1024,512]{1,0:T(8,128)(2,1)S(1)} %copy-done.5, f32[1024,512]{1,0:T(8,128)S(1)} %copy-done, bf16[256,512]{1,0:T(8,128)(2,1)S(1)} %copy-done.11, s32[1,128]{1,0:T(1,128)S(1)} %bitcast.7, f32[768,256]{1,0:T(8,128)S(1)} %copy-done.6, ...), custom_call_target="tpu_custom_call" | custom-call | tf_op jit(solution)/shard_map/send_out/pallas_call | solution.py:502
  220.4 3.4 %finish.1 = (bf16[2,1024,256]{2,1,0:T(8,128)(2,1)}, bf16[2,1024,256]{2,1,0:T(8,128)(2,1)}, f32[6,256]{1,0:T(8,128)}, f32[2,256]{1,0:T(2,128)}, f32[4,256]{1,0:T(...) custom-call(bf16[1024,512]{1,0:T(8,128)(2,1)S(1)} %get-tuple-element.57.nf_got, ...), custom_call_target="tpu_custom_call" | custom-call | tf_op jit(solution)/shard_map/finish/pallas_call | solution.py:554
  (38 shorter events, 4.6 us)
Async XLA Ops:
  0.6 1.2 copy-start.3
  1.9 1.2 copy-start.4
  3.1 0.7 copy-start.16
  3.8 0.7 copy-start.20
  4.5 0.7 copy-start.21
  5.8 0.7 copy-start.24
  6.5 0.7 copy-start.25
  60.8 1.0 copy-start.1
  61.8 1.0 copy-start.2
  62.7 0.7 copy-start.8
  63.5 0.7 copy-start.9
  64.2 0.7 copy-start.10
  64.9 0.7 copy-start.14
  65.6 0.7 copy-start.15
  66.8 105.3 %copy-start.23 = (s32[128]{0:T(128)S(1)}, s32[128]{0:T(128)}, u32[]{:S(2)}) copy-start(s32[128]{0:T(128)} %param.20) | copy-start | bytes 1540
  66.8 153.5 %copy-start.17 = (s32[1024]{0:T(1024)S(1)}, s32[1024]{0:T(1024)}, u32[]{:S(2)}) copy-start(s32[1024]{0:T(1024)} %param.17) | copy-start | bytes 12292
  172.1 1.6 copy-start
  173.7 1.2 copy-start.5
  174.9 1.1 copy-start.6
  176.1 1.0 copy-start.7
  177.1 0.9 copy-start.11
  178.1 0.9 copy-start.12
  179.0 0.9 copy-start.13
  180.0 0.7 copy-start.18
  (5 other events, 3.2 us)
